TPU v7x, 32 devices: a whole 2x2x4 slice. The times are simulated.
32 devices in a mesh: loop: 4 (over z), grp: 8 (over y, x, core).
Axes of the slice: x: 2, y: 2, z: 4, core: 2. Of those that a mesh axis runs over, the one named last changes fastest.
Arguments:
- images: bfloat16 [4096, 1152], P(('loop', 'grp')), may hold values from -0.1796875 to 0.1796875
- texts: bfloat16 [4096, 1152], P(('loop', 'grp')), may hold values from -0.1796875 to 0.1796875
- log_scale: float32 [], replicated, may hold values from 1.6 to 2.6
- bias: float32 [], replicated, may hold values from -6 to -2
Outputs:
- image_grad: float32 [4096, 1152], P(('loop', 'grp'))
- text_grad: float32 [4096, 1152], P(('loop', 'grp'))
All inputs are finite; a program needn't handle non-finite values.
Results may differ from a plain program's by a relative error of at most 0.0045.
Values may be sent and summed in bfloat16 or wider, within the bound.
A program may use at most 64 MiB of HBM per device.

v0:
```python
import jax
import jax.numpy as jnp
from jax import lax
from jax.sharding import PartitionSpec as P

WIN = 8


def passed_along(value, axis, steps):
    count = lax.axis_size(axis)
    pairs = [(source, (source + steps) % count) for source in range(count)]
    return lax.ppermute(value, axis, pairs)


def normalize(values):
    full = values.astype(jnp.float32)
    inverse = lax.rsqrt(jnp.sum(full * full, axis=-1, keepdims=True) + 1e-06)
    return (full * inverse, inverse)


def unnormalize(unit, inverse, grad):
    return inverse * (grad - unit * jnp.sum(unit * grad, axis=-1, keepdims=True))


def per_device(images, texts, log_scale, bias):
    rows = images.shape[0]
    width = images.shape[1]
    window = WIN
    image_unit, image_inv = normalize(images)
    text_unit, text_inv = normalize(texts)
    image_bf = image_unit.astype(jnp.bfloat16)
    text_bf = text_unit.astype(jnp.bfloat16)
    scale = jnp.exp(log_scale)
    columns = lax.broadcasted_iota(jnp.int32, (rows, rows), 1)
    row_ids = lax.broadcasted_iota(jnp.int32, (rows, rows), 0)
    matched = columns == row_ids
    image_acc = jnp.zeros((rows, width), jnp.float32)
    shard = text_bf
    carried = jnp.zeros((rows, width), jnp.float32)
    for step in range(window):
        logits = lax.dot_general(
            shard, image_bf, (((1,), (1,)), ((), ())), preferred_element_type=jnp.float32
        )
        level = scale * logits + bias
        if step == 0:
            sign = jnp.where(matched, 1.0, -1.0).astype(jnp.float32)
        else:
            sign = jnp.float32(-1.0)
        score_weights = (scale * -sign * jax.nn.sigmoid(-sign * level)).astype(jnp.bfloat16)
        image_part = lax.dot_general(
            score_weights, shard, (((0,), (0,)), ((), ())), preferred_element_type=jnp.float32
        )
        text_part = jnp.dot(score_weights, image_bf, preferred_element_type=jnp.float32)
        image_acc = image_acc + image_part
        carried = carried + text_part
        if step + 1 < window:
            shard = passed_along(shard, ("loop", "grp"), 1)
            carried = passed_along(carried, ("loop", "grp"), 1)
    text_acc = passed_along(carried, ("loop", "grp"), 1 - window)
    image_grad = unnormalize(image_unit, image_inv, image_acc)
    text_grad = unnormalize(text_unit, text_inv, text_acc)
    return (image_grad, text_grad)


def solution(mesh):
    return jax.shard_map(
        per_device,
        mesh=mesh,
        in_specs=(P(("loop", "grp"), None), P(("loop", "grp"), None), P(), P()),
        out_specs=(P(("loop", "grp"), None), P(("loop", "grp"), None)),
        check_vma=False,
    )
```

profile of v0, /device:TPU:0, one launch (start us, length us, event | category | flops | bytes accessed | tf_op | source)
XLA Modules:
  0.0 119.0 jit_solution(4713481763080405052)
XLA Ops:
  0.6 1.1 fusion.66
  1.8 0.1 fusion.70
  2.0 0.1 fusion.59
  3.4 0.3 fusion.49
  3.8 0.3 fusion.84
  4.1 0.5 collective-permute-start.7
  4.6 2.6 %collective-permute-start = (bf16[128,1152]{1,0:T(8,128)(2,1)S(1)}, bf16[128,1152]{1,0:T(8,128)(2,1)S(1)}, u32[]{:S(2)}, u32[]{:S(2)}) collective-permute-start(bf16[128,1152]{1,0:T(8,128)(2,1)S(1)} %fusion.59), channel_id=1, source_target_pairs={{0,1},{1,2},{2,3},{3,4},{4,5},{5,6},{6,7},{7,8},{8,9},{9,10},{10,1... | collective-permute-start | bytes 884744 | tf_op jit(solution)/shard_map/ppermute | solution.py:12
  7.2 0.3 fusion.94
  7.5 13.8 %collective-permute-done = bf16[128,1152]{1,0:T(8,128)(2,1)S(1)} collective-permute-done((bf16[128,1152]{1,0:T(8,128)(2,1)S(1)}, bf16[128,1152]{1,0:T(8,128)(2,1)S(1)}, u32[]{:S(2)}, u32[]{:S(2)}) %collective-permute-start) | collective-permute-done | bytes 294944 | tf_op jit(solution)/shard_map/ppermute | solution.py:12
  21.3 0.3 fusion.50
  21.6 0.3 convolution_add_fusion
  22.0 0.3 convolution_add_fusion.7
  22.3 8.7 %collective-permute-done.1 = bf16[128,1152]{1,0:T(8,128)(2,1)S(1)} collective-permute-done((bf16[128,1152]{1,0:T(8,128)(2,1)S(1)}, bf16[128,1152]{1,0:T(8,128)(2,1)S(1)}, u32[]{:S(2)}, u32[]{:S(2)}) %collective-permute-start.1) | collective-permute-done | bytes 294944 | tf_op jit(solution)/shard_map/ppermute | solution.py:12
  31.0 0.3 fusion.51
  31.4 0.3 fusion.81
  31.7 5.7 %collective-permute-done.8 = f32[128,1152]{1,0:T(8,128)S(1)} collective-permute-done((f32[128,1152]{1,0:T(8,128)S(1)}, f32[128,1152]{1,0:T(8,128)S(1)}, u32[]{:S(2)}, u32[]{:S(2)}) %collective-permute-start.8) | collective-permute-done | bytes 589856 | tf_op jit(solution)/shard_map/ppermute | solution.py:12
  37.3 0.1 add.143
  37.4 0.3 convolution_add_fusion.6
  37.7 3.0 %collective-permute-done.2 = bf16[128,1152]{1,0:T(8,128)(2,1)S(1)} collective-permute-done((bf16[128,1152]{1,0:T(8,128)(2,1)S(1)}, bf16[128,1152]{1,0:T(8,128)(2,1)S(1)}, u32[]{:S(2)}, u32[]{:S(2)}) %collective-permute-start.2) | collective-permute-done | bytes 294944 | tf_op jit(solution)/shard_map/ppermute | solution.py:12
  40.7 0.3 fusion.52
  41.1 0.3 fusion.79
  41.4 8.9 %collective-permute-done.9 = f32[128,1152]{1,0:T(8,128)S(1)} collective-permute-done((f32[128,1152]{1,0:T(8,128)S(1)}, f32[128,1152]{1,0:T(8,128)S(1)}, u32[]{:S(2)}, u32[]{:S(2)}) %collective-permute-start.9) | collective-permute-done | bytes 589856 | tf_op jit(solution)/shard_map/ppermute | solution.py:12
  50.3 0.1 add.144
  50.5 0.3 convolution_add_fusion.5
  50.7 2.8 %collective-permute-done.3 = bf16[128,1152]{1,0:T(8,128)(2,1)S(1)} collective-permute-done((bf16[128,1152]{1,0:T(8,128)(2,1)S(1)}, bf16[128,1152]{1,0:T(8,128)(2,1)S(1)}, u32[]{:S(2)}, u32[]{:S(2)}) %collective-permute-start.3) | collective-permute-done | bytes 294944 | tf_op jit(solution)/shard_map/ppermute | solution.py:12
  53.5 0.3 fusion.53
  53.9 0.3 fusion.77
  54.2 9.2 %collective-permute-done.10 = f32[128,1152]{1,0:T(8,128)S(1)} collective-permute-done((f32[128,1152]{1,0:T(8,128)S(1)}, f32[128,1152]{1,0:T(8,128)S(1)}, u32[]{:S(2)}, u32[]{:S(2)}) %collective-permute-start.10) | collective-permute-done | bytes 589856 | tf_op jit(solution)/shard_map/ppermute | solution.py:12
  63.5 0.3 convolution_add_fusion.4
  63.8 2.8 %collective-permute-done.4 = bf16[128,1152]{1,0:T(8,128)(2,1)S(1)} collective-permute-done((bf16[128,1152]{1,0:T(8,128)(2,1)S(1)}, bf16[128,1152]{1,0:T(8,128)(2,1)S(1)}, u32[]{:S(2)}, u32[]{:S(2)}) %collective-permute-start.4) | collective-permute-done | bytes 294944 | tf_op jit(solution)/shard_map/ppermute | solution.py:12
  66.5 0.3 fusion.54
  66.9 0.3 fusion.75
  67.2 9.2 %collective-permute-done.11 = f32[128,1152]{1,0:T(8,128)S(1)} collective-permute-done((f32[128,1152]{1,0:T(8,128)S(1)}, f32[128,1152]{1,0:T(8,128)S(1)}, u32[]{:S(2)}, u32[]{:S(2)}) %collective-permute-start.11) | collective-permute-done | bytes 589856 | tf_op jit(solution)/shard_map/ppermute | solution.py:12
  76.5 0.3 convolution_add_fusion.3
  76.8 2.8 %collective-permute-done.5 = bf16[128,1152]{1,0:T(8,128)(2,1)S(1)} collective-permute-done((bf16[128,1152]{1,0:T(8,128)(2,1)S(1)}, bf16[128,1152]{1,0:T(8,128)(2,1)S(1)}, u32[]{:S(2)}, u32[]{:S(2)}) %collective-permute-start.5) | collective-permute-done | bytes 294944 | tf_op jit(solution)/shard_map/ppermute | solution.py:12
  79.5 0.3 fusion.55
  79.9 0.3 fusion.73
  80.2 9.2 %collective-permute-done.12 = f32[128,1152]{1,0:T(8,128)S(1)} collective-permute-done((f32[128,1152]{1,0:T(8,128)S(1)}, f32[128,1152]{1,0:T(8,128)S(1)}, u32[]{:S(2)}, u32[]{:S(2)}) %collective-permute-start.12) | collective-permute-done | bytes 589856 | tf_op jit(solution)/shard_map/ppermute | solution.py:12
  89.5 0.3 convolution_add_fusion.2
  89.8 2.8 %collective-permute-done.6 = bf16[128,1152]{1,0:T(8,128)(2,1)S(1)} collective-permute-done((bf16[128,1152]{1,0:T(8,128)(2,1)S(1)}, bf16[128,1152]{1,0:T(8,128)(2,1)S(1)}, u32[]{:S(2)}, u32[]{:S(2)}) %collective-permute-start.6) | collective-permute-done | bytes 294944 | tf_op jit(solution)/shard_map/ppermute | solution.py:12
  92.6 0.3 fusion.56
  92.9 0.3 fusion.71
  93.2 14.2 %collective-permute-done.13 = f32[128,1152]{1,0:T(8,128)S(1)} collective-permute-done((f32[128,1152]{1,0:T(8,128)S(1)}, f32[128,1152]{1,0:T(8,128)S(1)}, u32[]{:S(2)}, u32[]{:S(2)}) %collective-permute-start.13) | collective-permute-done | bytes 589856 | tf_op jit(solution)/shard_map/ppermute | solution.py:12
  107.5 0.4 fusion.63
  107.9 1.0 fusion.65
  109.0 8.8 %collective-permute-done.14 = f32[128,1152]{1,0:T(8,128)S(1)} collective-permute-done((f32[128,1152]{1,0:T(8,128)S(1)}, f32[128,1152]{1,0:T(8,128)S(1)}, u32[]{:S(2)}, u32[]{:S(2)}) %collective-permute-start.14) | collective-permute-done | bytes 589856 | tf_op jit(solution)/shard_map/ppermute | solution.py:12
  117.7 0.2 fusion.67
  118.0 1.0 fusion.69
  (24 shorter events, 0.7 us)
Async XLA Ops:
  0.6 1.2 copy-start.1
  1.9 1.5 %copy-start = (bf16[128,1152]{1,0:T(8,128)(2,1)S(1)}, bf16[128,1152]{1,0:T(8,128)(2,1)}, u32[]{:S(2)}) copy-start(bf16[128,1152]{1,0:T(8,128)(2,1)} %param.4) | copy-start | bytes 884740
  4.1 17.5 %collective-permute-start.7 = (f32[128,1152]{1,0:T(8,128)S(1)}, f32[128,1152]{1,0:T(8,128)S(1)}, u32[]{:S(2)}, u32[]{:S(2)}) collective-permute-start(f32[128,1152]{1,0:T(8,128)S(1)} %fusion.84), channel_id=1, source_target_pairs={{0,1},{1,2},{2,3},{3,4},{4,5},{5,6},{6,7},{7,8},{8,9},{9,10},{10,1... | collective-permute-start | bytes 1769480 | tf_op jit(solution)/shard_map/ppermute | solution.py:12
  4.6 16.6 %collective-permute-start = (bf16[128,1152]{1,0:T(8,128)(2,1)S(1)}, bf16[128,1152]{1,0:T(8,128)(2,1)S(1)}, u32[]{:S(2)}, u32[]{:S(2)}) collective-permute-start(bf16[128,1152]{1,0:T(8,128)(2,1)S(1)} %fusion.59), channel_id=1, source_target_pairs={{0,1},{1,2},{2,3},{3,4},{4,5},{5,6},{6,7},{7,8},{8,9},{9,10},{10,1... | collective-permute-start | bytes 884744 | tf_op jit(solution)/shard_map/ppermute | solution.py:12
  21.3 9.7 %collective-permute-start.1 = (bf16[128,1152]{1,0:T(8,128)(2,1)S(1)}, bf16[128,1152]{1,0:T(8,128)(2,1)S(1)}, u32[]{:S(2)}, u32[]{:S(2)}) collective-permute-start(bf16[128,1152]{1,0:T(8,128)(2,1)S(1)} %collective-permute-done), channel_id=1, source_target_pairs={{0,1},{1,2},{2,3},{3,4},{4,5},{5,6},{6,7},{7,8},{8,9},{9,10},{10,1... | collective-permute-start | bytes 884744 | tf_op jit(solution)/shard_map/ppermute | solution.py:12
  21.9 15.4 %collective-permute-start.8 = (f32[128,1152]{1,0:T(8,128)S(1)}, f32[128,1152]{1,0:T(8,128)S(1)}, u32[]{:S(2)}, u32[]{:S(2)}) collective-permute-start(f32[128,1152]{1,0:T(8,128)S(1)} %convolution_add_fusion), channel_id=1, source_target_pairs={{0,1},{1,2},{2,3},{3,4},{4,5},{5,6},{6,7},{7,8},{8,9},{9,10},{10,1... | collective-permute-start | bytes 1769480 | tf_op jit(solution)/shard_map/ppermute | solution.py:12
  31.0 9.7 %collective-permute-start.2 = (bf16[128,1152]{1,0:T(8,128)(2,1)S(1)}, bf16[128,1152]{1,0:T(8,128)(2,1)S(1)}, u32[]{:S(2)}, u32[]{:S(2)}) collective-permute-start(bf16[128,1152]{1,0:T(8,128)(2,1)S(1)} %collective-permute-done.1), channel_id=1, source_target_pairs={{0,1},{1,2},{2,3},{3,4},{4,5},{5,6},{6,7},{7,8},{8,9},{9,10},{10,1... | collective-permute-start | bytes 884744 | tf_op jit(solution)/shard_map/ppermute | solution.py:12
  37.4 13.0 %collective-permute-start.9 = (f32[128,1152]{1,0:T(8,128)S(1)}, f32[128,1152]{1,0:T(8,128)S(1)}, u32[]{:S(2)}, u32[]{:S(2)}) collective-permute-start(f32[128,1152]{1,0:T(8,128)S(1)} %add.143), channel_id=1, source_target_pairs={{0,1},{1,2},{2,3},{3,4},{4,5},{5,6},{6,7},{7,8},{8,9},{9,10},{10,1... | collective-permute-start | bytes 1769480 | tf_op jit(solution)/shard_map/ppermute | solution.py:12
  40.7 12.8 %collective-permute-start.3 = (bf16[128,1152]{1,0:T(8,128)(2,1)S(1)}, bf16[128,1152]{1,0:T(8,128)(2,1)S(1)}, u32[]{:S(2)}, u32[]{:S(2)}) collective-permute-start(bf16[128,1152]{1,0:T(8,128)(2,1)S(1)} %collective-permute-done.2), channel_id=1, source_target_pairs={{0,1},{1,2},{2,3},{3,4},{4,5},{5,6},{6,7},{7,8},{8,9},{9,10},{10,1... | collective-permute-start | bytes 884744 | tf_op jit(solution)/shard_map/ppermute | solution.py:12
  50.4 13.0 %collective-permute-start.10 = (f32[128,1152]{1,0:T(8,128)S(1)}, f32[128,1152]{1,0:T(8,128)S(1)}, u32[]{:S(2)}, u32[]{:S(2)}) collective-permute-start(f32[128,1152]{1,0:T(8,128)S(1)} %add.144), channel_id=1, source_target_pairs={{0,1},{1,2},{2,3},{3,4},{4,5},{5,6},{6,7},{7,8},{8,9},{9,10},{10,1... | collective-permute-start | bytes 1769480 | tf_op jit(solution)/shard_map/ppermute | solution.py:12
  53.5 13.0 %collective-permute-start.4 = (bf16[128,1152]{1,0:T(8,128)(2,1)S(1)}, bf16[128,1152]{1,0:T(8,128)(2,1)S(1)}, u32[]{:S(2)}, u32[]{:S(2)}) collective-permute-start(bf16[128,1152]{1,0:T(8,128)(2,1)S(1)} %collective-permute-done.3), channel_id=1, source_target_pairs={{0,1},{1,2},{2,3},{3,4},{4,5},{5,6},{6,7},{7,8},{8,9},{9,10},{10,1... | collective-permute-start | bytes 884744 | tf_op jit(solution)/shard_map/ppermute | solution.py:12
  63.4 13.0 %collective-permute-start.11 = (f32[128,1152]{1,0:T(8,128)S(1)}, f32[128,1152]{1,0:T(8,128)S(1)}, u32[]{:S(2)}, u32[]{:S(2)}) collective-permute-start(f32[128,1152]{1,0:T(8,128)S(1)} %add.145), channel_id=1, source_target_pairs={{0,1},{1,2},{2,3},{3,4},{4,5},{5,6},{6,7},{7,8},{8,9},{9,10},{10,1... | collective-permute-start | bytes 1769480 | tf_op jit(solution)/shard_map/ppermute | solution.py:12
  66.5 13.0 %collective-permute-start.5 = (bf16[128,1152]{1,0:T(8,128)(2,1)S(1)}, bf16[128,1152]{1,0:T(8,128)(2,1)S(1)}, u32[]{:S(2)}, u32[]{:S(2)}) collective-permute-start(bf16[128,1152]{1,0:T(8,128)(2,1)S(1)} %collective-permute-done.4), channel_id=1, source_target_pairs={{0,1},{1,2},{2,3},{3,4},{4,5},{5,6},{6,7},{7,8},{8,9},{9,10},{10,1... | collective-permute-start | bytes 884744 | tf_op jit(solution)/shard_map/ppermute | solution.py:12
  76.4 13.0 %collective-permute-start.12 = (f32[128,1152]{1,0:T(8,128)S(1)}, f32[128,1152]{1,0:T(8,128)S(1)}, u32[]{:S(2)}, u32[]{:S(2)}) collective-permute-start(f32[128,1152]{1,0:T(8,128)S(1)} %add.146), channel_id=1, source_target_pairs={{0,1},{1,2},{2,3},{3,4},{4,5},{5,6},{6,7},{7,8},{8,9},{9,10},{10,1... | collective-permute-start | bytes 1769480 | tf_op jit(solution)/shard_map/ppermute | solution.py:12
  79.5 13.0 %collective-permute-start.6 = (bf16[128,1152]{1,0:T(8,128)(2,1)S(1)}, bf16[128,1152]{1,0:T(8,128)(2,1)S(1)}, u32[]{:S(2)}, u32[]{:S(2)}) collective-permute-start(bf16[128,1152]{1,0:T(8,128)(2,1)S(1)} %collective-permute-done.5), channel_id=1, source_target_pairs={{0,1},{1,2},{2,3},{3,4},{4,5},{5,6},{6,7},{7,8},{8,9},{9,10},{10,1... | collective-permute-start | bytes 884744 | tf_op jit(solution)/shard_map/ppermute | solution.py:12
  89.5 17.9 %collective-permute-start.13 = (f32[128,1152]{1,0:T(8,128)S(1)}, f32[128,1152]{1,0:T(8,128)S(1)}, u32[]{:S(2)}, u32[]{:S(2)}) collective-permute-start(f32[128,1152]{1,0:T(8,128)S(1)} %add.147), channel_id=1, source_target_pairs={{0,1},{1,2},{2,3},{3,4},{4,5},{5,6},{6,7},{7,8},{8,9},{9,10},{10,1... | collective-permute-start | bytes 1769480 | tf_op jit(solution)/shard_map/ppermute | solution.py:12
  107.5 10.3 %collective-permute-start.14 = (f32[128,1152]{1,0:T(8,128)S(1)}, f32[128,1152]{1,0:T(8,128)S(1)}, u32[]{:S(2)}, u32[]{:S(2)}) collective-permute-start(f32[128,1152]{1,0:T(8,128)S(1)} %add.148), channel_id=1, source_target_pairs={{0,25},{1,26},{2,27},{3,28},{4,29},{5,30},{6,31},{7,0},{8,1},{9,2}... | collective-permute-start | bytes 1769480 | tf_op jit(solution)/shard_map/ppermute | solution.py:12
where the time goes:
time: 119 us
  waiting for transfers between devices  102 us (86%)
  matrix products  7.34 us (6%)
  other arithmetic  4.09 us (3%)
  starting transfers between devices  3.53 us (3%)
  between operations  2.28 us (2%)
    ppermute x15, waiting for transfers between devices, passed_along(): return lax.ppermute(value, axis, pairs)  102 us
    ppermute x15, starting transfers between devices, passed_along(): return lax.ppermute(value, axis, pairs)  3.53 us
    dot_general x8, matrix products, per_device(): lax.dot_general(shard, image_bf, (((1,), (1,)), ((), ())), preferred_elem...  2.75 us
    dot_general x8, matrix products, per_device(): jnp.dot(score_weights, image_bf, preferred_element_type=jnp.float32)  2.41 us
  transfers between devices with their start and end apart: 15, of which 14 were waited for; matrix products, arithmetic and copies ran while one was open for 7% of the time, Pallas kernels for 0%

commit v1 on v0

v1 whole, which is shorter than its diff:
```python
import functools

import jax
import jax.numpy as jnp
from jax import lax
from jax.experimental import pallas as pl
from jax.experimental.pallas import tpu as pltpu
from jax.sharding import PartitionSpec as P

WIN = 8
MESH = pl.DeviceIdType.MESH
NT = (((1,), (1,)), ((), ()))


def kernel(
    n_loop, n_grp, images_ref, texts_ref, log_scale_ref, bias_ref, image_grad_ref, text_grad_ref,
    own, held, acc, send_sem, pass_sem, recv_sem,
):
    n = n_loop * n_grp
    me = lax.axis_index("loop") * n_grp + lax.axis_index("grp")
    core = lax.rem(me, 2)

    def place(steps):
        device = lax.rem(me + steps + n, n)
        return (device // n_grp, lax.rem(device, n_grp))

    sibling = place(1 - 2 * core)
    far = place(14 * core - 7)
    barrier = pltpu.get_barrier_semaphore()
    peers = [place(s) for s in (-6, -4, -2, 2, 4, 6)] + [sibling, far]
    for peer in peers:
        pl.semaphore_signal(barrier, inc=1, device_id=peer, device_id_type=MESH)

    def normalize(ref):
        full = ref[...].astype(jnp.float32)
        inverse = lax.rsqrt(jnp.sum(full * full, axis=-1, keepdims=True) + 1e-06)
        return full * inverse, inverse

    own[0] = normalize(texts_ref)[0].astype(jnp.bfloat16)
    own[1] = normalize(images_ref)[0].astype(jnp.bfloat16)
    pl.semaphore_wait(barrier, len(peers))

    def copy(source, kind, slot, send, device):
        return pltpu.make_async_remote_copy(
            src_ref=source, dst_ref=held.at[kind, slot], send_sem=send,
            recv_sem=recv_sem.at[kind, slot], device_id=device, device_id_type=MESH,
        )

    sends = []
    for j in (3, 2, 1):
        for kind, way in ((0, 1), (1, -1)):
            sends.append(copy(own.at[kind], kind, 2 * j - 1, send_sem.at[kind, j], place(way * 2 * j)))
    up = place(1 + 6 * core)
    down = place(-7 + 6 * core)
    sends.append(copy(own.at[0], 0, 6 * core, send_sem.at[0, 0], up))
    sends.append(copy(own.at[1], 1, 6 - 6 * core, send_sem.at[1, 0], down))
    for one in sends:
        one.start()

    scale = jnp.exp(jnp.full((1, 128), log_scale_ref[0], jnp.float32))
    bias = bias_ref[0]

    def step(kind, block, matched):
        logits = lax.dot_general(own[1 - kind], block, NT, preferred_element_type=jnp.float32)
        level = scale * logits + bias
        if matched:
            rows = lax.broadcasted_iota(jnp.int32, level.shape, 0)
            columns = lax.broadcasted_iota(jnp.int32, level.shape, 1)
            sign = jnp.where(rows == columns, 1.0, -1.0)
            weights = scale * -sign * jax.nn.sigmoid(-sign * level)
        else:
            weights = scale * jax.nn.sigmoid(level)
        part = jnp.dot(weights.astype(jnp.bfloat16), block, preferred_element_type=jnp.float32)
        acc[kind] = part if matched else acc[kind] + part

    for kind in range(2):
        step(kind, own[kind], True)

    passes = []
    for j in (1, 2, 3):
        for kind in range(2):
            copy(own.at[kind], kind, 2 * j - 1, send_sem.at[kind, j], sibling).wait_recv()
            lean = core if kind == 0 else 1 - core
            one = copy(held.at[kind, 2 * j - 1], kind, 2 * j - 2 * lean, pass_sem.at[kind, j - 1], sibling)
            one.start()
            passes.append(one)
            step(kind, held[kind, 2 * j - 1], False)
    for slot in (0, 2, 4, 6):
        for kind in range(2):
            copy(own.at[kind], kind, slot, send_sem.at[kind, 0], sibling).wait_recv()
            step(kind, held[kind, slot], False)

    for source, kind, out in ((images_ref, 0, image_grad_ref), (texts_ref, 1, text_grad_ref)):
        unit, inverse = normalize(source)
        grad = acc[kind]
        out[...] = inverse * (grad - unit * jnp.sum(unit * grad, axis=-1, keepdims=True))
    for one in sends + passes:
        one.wait_send()


def per_device(n_loop, n_grp, images, texts, log_scale, bias):
    rows, width = images.shape
    vmem = pl.BlockSpec(memory_space=pltpu.VMEM)
    smem = pl.BlockSpec(memory_space=pltpu.SMEM)
    grad = jax.ShapeDtypeStruct((rows, width), jnp.float32)
    return pl.pallas_call(
        functools.partial(kernel, n_loop, n_grp),
        out_shape=(grad, grad),
        in_specs=[vmem, vmem, smem, smem],
        out_specs=(vmem, vmem),
        scratch_shapes=[
            pltpu.VMEM((2, rows, width), jnp.bfloat16),
            pltpu.VMEM((2, WIN - 1, rows, width), jnp.bfloat16),
            pltpu.VMEM((2, rows, width), jnp.float32),
            pltpu.SemaphoreType.DMA((2, 4)),
            pltpu.SemaphoreType.DMA((2, 3)),
            pltpu.SemaphoreType.DMA((2, WIN - 1)),
        ],
        compiler_params=pltpu.CompilerParams(
            collective_id=0, has_side_effects=True, vmem_limit_bytes=32 * 1024 * 1024
        ),
    )(images, texts, log_scale.reshape(1), bias.reshape(1))


def solution(mesh):
    rows = P(("loop", "grp"), None)
    return jax.shard_map(
        functools.partial(per_device, mesh.shape["loop"], mesh.shape["grp"]),
        mesh=mesh,
        in_specs=(rows, rows, P(), P()),
        out_specs=(rows, rows),
        check_vma=False,
    )
```

time: 119 us -> 47.8 us (0.40)
  waiting for transfers between devices: 102 us -> 0 us
  Pallas kernels: 0 us -> 42.1 us
  matrix products: 7.34 us -> 0 us
  other arithmetic: 4.09 us -> 0 us
  local copies, waits for them, and re-layouts: 0.01 us -> 3.55 us
  starting transfers between devices: 3.53 us -> 0 us
    ppermute x15 -> x0, waiting for transfers between devices: 102 us -> none  [passed_along(): return lax.ppermute(value, axis, pairs)]
    pallas_call x0 -> x1, Pallas kernels: none -> 42.1 us  [per_device(): pl.pallas_call(functools.partial(kernel, n_loop, n_grp), out_shape=(grad,...]
    dot_general x24 -> x0, matrix products: 7.34 us -> none  [the longest x8 2.75 us: per_device(): lax.dot_general(shard, image_bf, (((1,), (1,)), ((), ())), preferred_elem...]
    unnamed x4 -> x6, local copies, waits for them, and re-layouts: 0.01 us -> 3.55 us
    ppermute x15 -> x0, starting transfers between devices: 3.53 us -> none  [passed_along(): return lax.ppermute(value, axis, pairs)]
    mul x2 -> x0, other arithmetic: 2.07 us -> none  [unnormalize(): inverse * (grad - unit * jnp.sum(unit * grad, axis=-1, keepdims=True))]
    reduce_sum x3 -> x0, other arithmetic: 1.51 us -> none  [the longest x2 1.29 us: normalize(): inverse = lax.rsqrt(jnp.sum(full * full, axis=-1, keepdims=True) + 1e-06)]
  transfers between devices with their start and end apart: 15 -> 0, of which waited for: 14 -> 0; matrix products, arithmetic and copies ran while one was open for 7% -> 0% of each run, Pallas kernels for 0% -> 0%
where the time goes in v1:
time: 47.8 us; the launch traced here: 47.6 us
  Pallas kernels  42.1 us (88%)
  local copies, waits for them, and re-layouts  3.55 us (7%)
  between operations  1.94 us (4%)
    pallas_call x1, Pallas kernels, per_device(): pl.pallas_call(functools.partial(kernel, n_loop, n_grp), out_shape=(grad,...  42.1 us
    unnamed x6, local copies, waits for them, and re-layouts  3.55 us

profile of v1, /device:TPU:0, one launch (start us, length us, event | category | flops | bytes accessed | tf_op | source)
XLA Modules:
  0.0 47.6 jit_solution(11506106653051378715)
XLA Ops:
  1.9 0.0 copy-start
  1.9 1.0 %copy-done = bf16[128,1152]{1,0:T(8,128)(2,1)S(1)} copy-done((bf16[128,1152]{1,0:T(8,128)(2,1)S(1)}, bf16[128,1152]{1,0:T(8,128)(2,1)}, u32[]{:S(2)}) %copy-start) | copy-done | bytes 294936
  2.9 0.0 copy-start.1
  2.9 1.0 %copy-done.1 = bf16[128,1152]{1,0:T(8,128)(2,1)S(1)} copy-done((bf16[128,1152]{1,0:T(8,128)(2,1)S(1)}, bf16[128,1152]{1,0:T(8,128)(2,1)}, u32[]{:S(2)}) %copy-start.1) | copy-done | bytes 294936
  3.8 42.1 %shard_map.59 = (f32[128,1152]{1,0:T(8,128)S(1)}, f32[128,1152]{1,0:T(8,128)S(1)}) custom-call(bf16[128,1152]{1,0:T(8,128)(2,1)S(1)} %copy-done, bf16[128,1152]{1,0:T(8,128)(2,1)S(1)} %copy-done.1, f32[1]{0:T(128)} %bitcast.2.log_scale_ref, f32[1]{0:T(128)} %bitcast.3.bias_ref), custom_call_target="tpu_custom_call" | custom-call | tf_op jit(solution)/shard_map/pallas_call | solution.py:106
  45.9 0.8 %copy.10 = f32[128,1152]{1,0:T(8,128)} copy(f32[128,1152]{1,0:T(8,128)S(1)} %get-tuple-element.4) | data formatting | bytes 1179648
  46.7 0.8 %copy.11 = f32[128,1152]{1,0:T(8,128)} copy(f32[128,1152]{1,0:T(8,128)S(1)} %get-tuple-element.5) | data formatting | bytes 1179648
Async XLA Ops:
  1.9 1.0 %copy-start = (bf16[128,1152]{1,0:T(8,128)(2,1)S(1)}, bf16[128,1152]{1,0:T(8,128)(2,1)}, u32[]{:S(2)}) copy-start(bf16[128,1152]{1,0:T(8,128)(2,1)} %images_ref.1) | copy-start | bytes 884740
  2.9 1.0 %copy-start.1 = (bf16[128,1152]{1,0:T(8,128)(2,1)S(1)}, bf16[128,1152]{1,0:T(8,128)(2,1)}, u32[]{:S(2)}) copy-start(bf16[128,1152]{1,0:T(8,128)(2,1)} %texts_ref.1) | copy-start | bytes 884740

commit v2 on v1

v2 whole, which is shorter than its diff:
```python
import functools

import jax
import jax.numpy as jnp
from jax import lax
from jax.experimental import pallas as pl
from jax.experimental.pallas import tpu as pltpu
from jax.sharding import PartitionSpec as P

WIN = 8
MESH = pl.DeviceIdType.MESH
NT = (((1,), (1,)), ((), ()))


def kernel(
    n_loop, n_grp, images_hbm, texts_hbm, log_scale_ref, bias_ref, image_grad_ref, text_grad_ref,
    raw, own, crossed, held, acc, load_sem, cross_send, cross_recv, send_sem, pass_sem, recv_sem,
):
    n = n_loop * n_grp
    me = lax.axis_index("loop") * n_grp + lax.axis_index("grp")
    bits = [lax.rem(me, 2), lax.rem(me // 2, 2), lax.rem(me // 4, 2)]
    top = [None] + [bits[r.bit_length() - 1] for r in range(1, WIN)]

    def place(device):
        return (device // n_grp, lax.rem(device, n_grp))

    def member(r):
        device = me
        for b in range(3):
            if r >> b & 1:
                device = device + (1 - 2 * bits[b]) * (1 << b)
        return place(device)

    above, below = place(lax.rem(me + WIN, n)), place(lax.rem(me - WIN + n, n))
    loads = [
        pltpu.make_async_copy(ref, raw.at[i], load_sem.at[i]) for i, ref in enumerate((texts_hbm, images_hbm))
    ]
    for one in loads:
        one.start()
    barrier = pltpu.get_barrier_semaphore()
    peers = [above, below] + [member(r) for r in (1, 2, 4, 6)]
    for peer in peers:
        pl.semaphore_signal(barrier, inc=1, device_id=peer, device_id_type=MESH)

    def normalize(kind):
        full = raw[kind].astype(jnp.float32)
        inverse = lax.rsqrt(jnp.sum(full * full, axis=-1, keepdims=True) + 1e-06)
        return full * inverse, inverse

    for kind in range(2):
        loads[kind].wait()
        own[kind] = normalize(kind)[0].astype(jnp.bfloat16)
    pl.semaphore_wait(barrier, len(peers))

    def send(source, late, r, sem, device):
        return pltpu.make_async_remote_copy(
            src_ref=source, dst_ref=held.at[late, r - 1], send_sem=sem,
            recv_sem=recv_sem.at[late, r - 1], device_id=device, device_id_type=MESH,
        )

    crosses = [
        pltpu.make_async_remote_copy(
            src_ref=own.at[kind], dst_ref=crossed.at[kind], send_sem=cross_send.at[kind],
            recv_sem=cross_recv.at[kind], device_id=device, device_id_type=MESH,
        )
        for kind, device in ((0, above), (1, below))
    ]
    near = [send(own.at[top[r]], 0, r, send_sem.at[0, r - 1], member(r)) for r in (1, 2, 4, 6)]
    late = [send(crossed.at[1 - top[r]], 1, r, send_sem.at[1, r - 1], member(r)) for r in (1, 2, 4, 6)]
    for one in crosses + near:
        one.start()

    scale = jnp.exp(jnp.full((1, 128), log_scale_ref[0], jnp.float32))
    bias = bias_ref[0]

    def step(kind, block, matched=False):
        logits = lax.dot_general(own[1 - kind], block, NT, preferred_element_type=jnp.float32)
        level = scale * logits + bias
        if matched:
            rows = lax.broadcasted_iota(jnp.int32, level.shape, 0)
            columns = lax.broadcasted_iota(jnp.int32, level.shape, 1)
            sign = jnp.where(rows == columns, 1.0, -1.0)
            weights = scale * -sign * jax.nn.sigmoid(-sign * level)
        else:
            weights = scale * jax.nn.sigmoid(level)
        part = jnp.dot(weights.astype(jnp.bfloat16), block, preferred_element_type=jnp.float32)
        acc[kind] = part if matched else acc[kind] + part

    for kind in range(2):
        step(kind, own[kind], True)

    passes = []

    def arrived(is_late, r):
        send(own.at[0], is_late, r, send_sem.at[is_late, r - 1], member(1)).wait_recv()
        if r in (2, 4, 6):
            one = send(held.at[is_late, r - 1], is_late, r + 1, pass_sem.at[is_late, r // 2 - 1], member(1))
            one.start()
            passes.append(one)
        step(top[r] if is_late else 1 - top[r], held[is_late, r - 1])

    for r in (1, 2, 4):
        arrived(0, r)
    for one in crosses:
        one.wait_recv()
    for one in late:
        one.start()
    for r in (6, 3, 5, 7):
        arrived(0, r)
    for r in (1, 2, 4, 6, 3, 5, 7):
        arrived(1, r)

    for kind, out in ((1, image_grad_ref), (0, text_grad_ref)):
        unit, inverse = normalize(kind)
        grad = acc[1 - kind]
        out[...] = inverse * (grad - unit * jnp.sum(unit * grad, axis=-1, keepdims=True))
    for one in crosses + near + late + passes:
        one.wait_send()


def per_device(n_loop, n_grp, images, texts, log_scale, bias):
    rows, width = images.shape
    vmem = pl.BlockSpec(memory_space=pltpu.VMEM)
    smem = pl.BlockSpec(memory_space=pltpu.SMEM)
    hbm = pl.BlockSpec(memory_space=pl.ANY)
    grad = jax.ShapeDtypeStruct((rows, width), jnp.float32)
    dma = pltpu.SemaphoreType.DMA
    return pl.pallas_call(
        functools.partial(kernel, n_loop, n_grp),
        out_shape=(grad, grad),
        in_specs=[hbm, hbm, smem, smem],
        out_specs=(vmem, vmem),
        scratch_shapes=[
            pltpu.VMEM((2, rows, width), jnp.bfloat16),
            pltpu.VMEM((2, rows, width), jnp.bfloat16),
            pltpu.VMEM((2, rows, width), jnp.bfloat16),
            pltpu.VMEM((2, WIN - 1, rows, width), jnp.bfloat16),
            pltpu.VMEM((2, rows, width), jnp.float32),
            dma((2,)),
            dma((2,)),
            dma((2,)),
            dma((2, WIN - 1)),
            dma((2, 3)),
            dma((2, WIN - 1)),
        ],
        compiler_params=pltpu.CompilerParams(
            collective_id=0, has_side_effects=True, vmem_limit_bytes=48 * 1024 * 1024
        ),
    )(images, texts, log_scale.reshape(1), bias.reshape(1))


def solution(mesh):
    rows = P(("loop", "grp"), None)
    return jax.shard_map(
        functools.partial(per_device, mesh.shape["loop"], mesh.shape["grp"]),
        mesh=mesh,
        in_specs=(rows, rows, P(), P()),
        out_specs=(rows, rows),
        check_vma=False,
    )
```

time: 47.8 us -> 41.7 us (0.87)
  Pallas kernels: 42.1 us -> 36.1 us
    pallas_call x1, Pallas kernels: 42.1 us -> 36.1 us  [per_device(): pl.pallas_call(functools.partial(kernel, n_loop, n_grp), out_shape=(grad,...]
where the time goes in v2:
time: 41.7 us; the launch traced here: 41.5 us
  Pallas kernels  36.1 us (87%)
  local copies, waits for them, and re-layouts  3.55 us (9%)
  between operations  1.94 us (5%)
    pallas_call x1, Pallas kernels, per_device(): pl.pallas_call(functools.partial(kernel, n_loop, n_grp), out_shape=(grad,...  36.1 us
    unnamed x6, local copies, waits for them, and re-layouts  3.55 us

profile of v2, /device:TPU:0, one launch (start us, length us, event | category | flops | bytes accessed | tf_op | source)
XLA Modules:
  0.0 41.5 jit_solution(3703534686998309087)
XLA Ops:
  1.9 0.0 copy-start
  1.9 1.0 %copy-done = bf16[128,1152]{1,0:T(8,128)(2,1)S(1)} copy-done((bf16[128,1152]{1,0:T(8,128)(2,1)S(1)}, bf16[128,1152]{1,0:T(8,128)(2,1)}, u32[]{:S(2)}) %copy-start) | copy-done | bytes 294936
  2.9 0.0 copy-start.1
  2.9 1.0 %copy-done.1 = bf16[128,1152]{1,0:T(8,128)(2,1)S(1)} copy-done((bf16[128,1152]{1,0:T(8,128)(2,1)S(1)}, bf16[128,1152]{1,0:T(8,128)(2,1)}, u32[]{:S(2)}) %copy-start.1) | copy-done | bytes 294936
  3.8 36.1 %shard_map.59 = (f32[128,1152]{1,0:T(8,128)S(1)}, f32[128,1152]{1,0:T(8,128)S(1)}) custom-call(bf16[128,1152]{1,0:T(8,128)(2,1)S(1)} %copy-done, bf16[128,1152]{1,0:T(8,128)(2,1)S(1)} %copy-done.1, f32[1]{0:T(128)} %bitcast.2.log_scale_ref, f32[1]{0:T(128)} %bitcast.3.bias_ref), custom_call_target="tpu_custom_call" | custom-call | tf_op jit(solution)/shard_map/pallas_call | solution.py:128
  39.9 0.8 %copy.10 = f32[128,1152]{1,0:T(8,128)} copy(f32[128,1152]{1,0:T(8,128)S(1)} %get-tuple-element.4) | data formatting | bytes 1179648
  40.7 0.8 %copy.11 = f32[128,1152]{1,0:T(8,128)} copy(f32[128,1152]{1,0:T(8,128)S(1)} %get-tuple-element.5) | data formatting | bytes 1179648
Async XLA Ops:
  1.9 1.0 %copy-start = (bf16[128,1152]{1,0:T(8,128)(2,1)S(1)}, bf16[128,1152]{1,0:T(8,128)(2,1)}, u32[]{:S(2)}) copy-start(bf16[128,1152]{1,0:T(8,128)(2,1)} %images_hbm.1) | copy-start | bytes 884740
  2.9 1.0 %copy-start.1 = (bf16[128,1152]{1,0:T(8,128)(2,1)S(1)}, bf16[128,1152]{1,0:T(8,128)(2,1)}, u32[]{:S(2)}) copy-start(bf16[128,1152]{1,0:T(8,128)(2,1)} %texts_hbm.1) | copy-start | bytes 884740

commit v3 on v2

v3 whole, which is shorter than its diff:
```python
import functools

import jax
import jax.numpy as jnp
from jax import lax
from jax.experimental import pallas as pl
from jax.experimental.pallas import tpu as pltpu
from jax.sharding import PartitionSpec as P

WIN = 8
CHUNKS = 3
SIZES = (2, 2, 2, 2)
PARTS = len(SIZES)
ROUTES = ('CDDY', 'CDDY')
MESH = pl.DeviceIdType.MESH
NT = (((1,), (1,)), ((), ()))


def kernel(
    n_loop, n_grp, images_hbm, texts_hbm, log_scale_ref, bias_ref, image_grad_ref, text_grad_ref,
    raw, own, crossed, held, acc, load_sem, cross_send, cross_recv, send_sem, pass_sem, turn_sem, recv_sem,
):
    n = n_loop * n_grp
    wide = own.shape[2] // CHUNKS
    unit = images_hbm.shape[0] // 8
    offsets = [sum(SIZES[:h]) * unit for h in range(PARTS)]
    me = lax.axis_index("loop") * n_grp + lax.axis_index("grp")
    bits = [lax.rem(me, 2), lax.rem(me // 2, 2), lax.rem(me // 4, 2)]
    top = [None] + [bits[r.bit_length() - 1] for r in range(1, WIN)]

    def place(device):
        return (device // n_grp, lax.rem(device, n_grp))

    def member(r):
        device = me
        for b in range(3):
            if r >> b & 1:
                device = device + (1 - 2 * bits[b]) * (1 << b)
        return place(device)

    above, below = place(lax.rem(me + WIN, n)), place(lax.rem(me - WIN + n, n))
    loads = [
        pltpu.make_async_copy(ref, raw.at[i], load_sem.at[i]) for i, ref in enumerate((texts_hbm, images_hbm))
    ]
    for one in loads:
        one.start()
    barrier = pltpu.get_barrier_semaphore()
    peers = [above, below] + [member(r) for r in (1, 2, 4, 6)]
    for peer in peers:
        pl.semaphore_signal(barrier, inc=1, device_id=peer, device_id_type=MESH)

    def normalize(kind):
        full = raw[kind].astype(jnp.float32)
        inverse = lax.rsqrt(jnp.sum(full * full, axis=-1, keepdims=True) + 1e-06)
        return full * inverse, inverse

    for kind in range(2):
        loads[kind].wait()
        own[kind] = normalize(kind)[0].astype(jnp.bfloat16)
    pl.semaphore_wait(barrier, len(peers))

    def half(ref, h):
        return ref.at[pl.ds(offsets[h], SIZES[h] * unit)]

    def send(source, late, r, h, sem, device):
        return pltpu.make_async_remote_copy(
            src_ref=half(source, h), dst_ref=half(held.at[late, r - 1], h), send_sem=sem.at[late, r - 1, h],
            recv_sem=recv_sem.at[late, r - 1, h], device_id=device, device_id_type=MESH,
        )

    def cross(kind, h):
        return pltpu.make_async_remote_copy(
            src_ref=half(own.at[kind], h), dst_ref=half(crossed.at[kind], h), send_sem=cross_send.at[kind, h],
            recv_sem=cross_recv.at[kind, h], device_id=(above, below)[kind], device_id_type=MESH,
        )

    started = []

    def start(one):
        one.start()
        started.append(one)

    def spread(late, h):
        def block(r):
            return crossed.at[1 - top[r]] if late else own.at[top[r]]

        for r in (2, 4, 1):
            start(send(block(r), late, r, h, send_sem, member(r)))
        if ROUTES[late][h] == "C":
            start_if(send(block(6), late, 6, h, send_sem, member(6)))

    even = bits[1] * bits[2] + (1 - bits[1]) * (1 - bits[2])
    turn = place(me + even * (1 - 2 * bits[1]) * 2 + (1 - even) * (1 - 2 * bits[2]) * 4)
    started_if = []

    def start_if(one):
        @pl.when(even == 0)
        def _():
            one.start()

        started_if.append(one)

    def relay(late, h):
        route = ROUTES[late][h]
        if route == "Y":
            start(send(held.at[late, 3], late, 6, h, turn_sem, member(2)))
        elif route == "D":
            start(send(held.at[late, 1 + 2 * even], late, 6, h, turn_sem, turn))
        else:
            start_if(send(held.at[late, 1], late, 6, h, turn_sem, member(4)))

    def direct(late, h):
        for r in (2, 4):
            send(own.at[0], late, r, h, send_sem, member(1)).wait_recv()
        relay(late, h)
        for r in (2, 4):
            start(send(held.at[late, r - 1], late, r + 1, h, pass_sem, member(1)))

    scale = jnp.exp(jnp.full((1, 1), log_scale_ref[0], jnp.float32))
    bias = bias_ref[0]

    def step(kind, block, matched=False):
        def columns(ref, c):
            value = ref[..., c * wide : (c + 1) * wide]
            return value.reshape(-1, wide)

        logits = sum(
            lax.dot_general(columns(own.at[1 - kind], c), columns(block, c), NT, preferred_element_type=jnp.float32)
            for c in range(CHUNKS)
        )
        level = scale * logits + bias
        if matched:
            rows = lax.broadcasted_iota(jnp.int32, level.shape, 0)
            others = lax.broadcasted_iota(jnp.int32, level.shape, 1)
            sign = jnp.where(rows == others, 1.0, -1.0)
            weights = scale * -sign * jax.nn.sigmoid(-sign * level)
        else:
            weights = scale * jax.nn.sigmoid(level)
        weights = weights.astype(jnp.bfloat16)
        for c in range(CHUNKS):
            at = (kind, slice(None), slice(c * wide, (c + 1) * wide))
            part = jnp.dot(weights, columns(block, c), preferred_element_type=jnp.float32)
            acc[at] = part if matched else acc[at] + part

    for h in range(PARTS):
        for kind in range(2):
            start(cross(kind, h))
        spread(0, h)
    for kind in range(2):
        step(kind, own.at[kind], True)

    def arrived(late, *relations):
        for h in range(PARTS):
            for r in relations:
                send(own.at[0], late, r, h, send_sem, member(1)).wait_recv()
                if r == 6:
                    start(send(held.at[late, 5], late, 7, h, pass_sem, member(1)))

    def use(late, first, count):
        step(top[first] if late else 1 - top[first], held.at[late, pl.ds(first - 1, count)])

    def crossing(h):
        for kind in range(2):
            cross(kind, h).wait_recv()
        spread(1, h)

    arrived(0, 1)
    use(0, 1, 1)
    direct(0, 0)
    direct(0, 1)
    crossing(0)
    direct(0, 2)
    direct(0, 3)
    crossing(1)
    use(0, 2, 1)
    use(0, 4, 1)
    crossing(2)
    arrived(0, 3, 5)
    use(0, 3, 1)
    direct(1, 0)
    crossing(3)
    direct(1, 1)
    arrived(0, 6)
    direct(1, 2)
    use(0, 5, 1)
    direct(1, 3)
    arrived(1, 1)
    use(1, 1, 1)
    use(1, 2, 1)
    use(1, 4, 1)
    arrived(0, 7)
    use(0, 6, 2)
    arrived(1, 3, 5)
    arrived(1, 6)
    use(1, 3, 1)
    use(1, 5, 1)
    arrived(1, 7)
    use(1, 6, 2)
    for kind, out in ((1, image_grad_ref), (0, text_grad_ref)):
        unit, inverse = normalize(kind)
        grad = acc[1 - kind]
        out[...] = inverse * (grad - unit * jnp.sum(unit * grad, axis=-1, keepdims=True))
    for one in started:
        one.wait_send()

    @pl.when(even == 0)
    def _():
        for one in started_if:
            one.wait_send()


def per_device(n_loop, n_grp, images, texts, log_scale, bias):
    rows, width = images.shape
    vmem = pl.BlockSpec(memory_space=pltpu.VMEM)
    smem = pl.BlockSpec(memory_space=pltpu.SMEM)
    hbm = pl.BlockSpec(memory_space=pl.ANY)
    grad = jax.ShapeDtypeStruct((rows, width), jnp.float32)
    dma = pltpu.SemaphoreType.DMA
    return pl.pallas_call(
        functools.partial(kernel, n_loop, n_grp),
        out_shape=(grad, grad),
        in_specs=[hbm, hbm, smem, smem],
        out_specs=(vmem, vmem),
        scratch_shapes=[
            pltpu.VMEM((2, rows, width), jnp.bfloat16),
            pltpu.VMEM((2, rows, width), jnp.bfloat16),
            pltpu.VMEM((2, rows, width), jnp.bfloat16),
            pltpu.VMEM((2, WIN - 1, rows, width), jnp.bfloat16),
            pltpu.VMEM((2, rows, width), jnp.float32),
            dma((2,)),
            dma((2, PARTS)),
            dma((2, PARTS)),
            dma((2, WIN - 1, PARTS)),
            dma((2, WIN - 1, PARTS)),
            dma((2, WIN - 1, PARTS)),
            dma((2, WIN - 1, PARTS)),
        ],
        compiler_params=pltpu.CompilerParams(
            collective_id=0, has_side_effects=True, vmem_limit_bytes=48 * 1024 * 1024
        ),
    )(
        *(pltpu.with_memory_space_constraint(value, pltpu.HBM) for value in (images, texts)),
        log_scale.reshape(1),
        bias.reshape(1),
    )


def solution(mesh):
    rows = P(("loop", "grp"), None)
    return jax.shard_map(
        functools.partial(per_device, mesh.shape["loop"], mesh.shape["grp"]),
        mesh=mesh,
        in_specs=(rows, rows, P(), P()),
        out_specs=(rows, rows),
        check_vma=False,
    )
```

time: 41.7 us -> 37.1 us (0.89)
  Pallas kernels: 36.1 us -> 33.3 us
  local copies, waits for them, and re-layouts: 3.55 us -> 1.63 us
    pallas_call x1, Pallas kernels: 36.1 us -> 33.3 us  [per_device(): pl.pallas_call(functools.partial(kernel, n_loop, n_grp), out_shape=(grad,...]
    unnamed x6 -> x2, local copies, waits for them, and re-layouts: 3.55 us -> 1.63 us
where the time goes in v3:
time: 37.1 us; the launch traced here: 36.9 us
  Pallas kernels  33.3 us (90%)
  between operations  1.93 us (5%)
  local copies, waits for them, and re-layouts  1.63 us (4%)
    pallas_call x1, Pallas kernels, per_device(): pl.pallas_call(functools.partial(kernel, n_loop, n_grp), out_shape=(grad,...  33.3 us
    unnamed x2, local copies, waits for them, and re-layouts  1.63 us

profile of v3, /device:TPU:0, one launch (start us, length us, event | category | flops | bytes accessed | tf_op | source)
XLA Modules:
  0.0 36.9 jit_solution(15281066081121644356)
XLA Ops:
  1.9 33.3 %shard_map.59 = (f32[128,1152]{1,0:T(8,128)S(1)}, f32[128,1152]{1,0:T(8,128)S(1)}) custom-call(bf16[128,1152]{1,0:T(8,128)(2,1)} %images_hbm.1, bf16[128,1152]{1,0:T(8,128)(2,1)} %texts_hbm.1, f32[1]{0:T(128)} %bitcast.2.log_scale_ref, f32[1]{0:T(128)} %bitcast.3.bias_ref), custom_call_target="tpu_custom_call" | custom-call | tf_op jit(solution)/shard_map/pallas_call | solution.py:219
  35.2 0.8 %copy.10 = f32[128,1152]{1,0:T(8,128)} copy(f32[128,1152]{1,0:T(8,128)S(1)} %get-tuple-element.4) | data formatting | bytes 1179648
  36.0 0.8 %copy.11 = f32[128,1152]{1,0:T(8,128)} copy(f32[128,1152]{1,0:T(8,128)S(1)} %get-tuple-element.5) | data formatting | bytes 1179648

commit v4 on v3

--- a/solution.py
+++ b/solution.py
@@ -54,9 +54,12 @@
         inverse = lax.rsqrt(jnp.sum(full * full, axis=-1, keepdims=True) + 1e-06)
         return full * inverse, inverse
 
+    inverses = []
     for kind in range(2):
         loads[kind].wait()
-        own[kind] = normalize(kind)[0].astype(jnp.bfloat16)
+        unit_rows, inverse = normalize(kind)
+        own[kind] = unit_rows.astype(jnp.bfloat16)
+        inverses.append(inverse)
     pl.semaphore_wait(barrier, len(peers))
 
     def half(ref, h):
@@ -197,7 +200,8 @@
     arrived(1, 7)
     use(1, 6, 2)
     for kind, out in ((1, image_grad_ref), (0, text_grad_ref)):
-        unit, inverse = normalize(kind)
+        inverse = inverses[kind]
+        unit = raw[kind].astype(jnp.float32) * inverse
         grad = acc[1 - kind]
         out[...] = inverse * (grad - unit * jnp.sum(unit * grad, axis=-1, keepdims=True))
     for one in started:

time: 37.1 us -> 37.1 us (level)
  no operation moved by 1% of the time
where the time goes in v4:
time: 37.1 us; the launch traced here: 36.8 us
  Pallas kernels  33.3 us (90%)
  between operations  1.93 us (5%)
  local copies, waits for them, and re-layouts  1.63 us (4%)
    pallas_call x1, Pallas kernels, per_device(): pl.pallas_call(functools.partial(kernel, n_loop, n_grp), out_shape=(grad,...  33.3 us
    unnamed x2, local copies, waits for them, and re-layouts  1.63 us

profile of v4, /device:TPU:0, one launch (start us, length us, event | category | flops | bytes accessed | tf_op | source)
XLA Modules:
  0.0 36.8 jit_solution(801760372593175150)
XLA Ops:
  1.9 33.3 %shard_map.59 = (f32[128,1152]{1,0:T(8,128)S(1)}, f32[128,1152]{1,0:T(8,128)S(1)}) custom-call(bf16[128,1152]{1,0:T(8,128)(2,1)} %images_hbm.1, bf16[128,1152]{1,0:T(8,128)(2,1)} %texts_hbm.1, f32[1]{0:T(128)} %bitcast.2.log_scale_ref, f32[1]{0:T(128)} %bitcast.3.bias_ref), custom_call_target="tpu_custom_call" | custom-call | tf_op jit(solution)/shard_map/pallas_call | solution.py:223
  35.2 0.8 %copy.10 = f32[128,1152]{1,0:T(8,128)} copy(f32[128,1152]{1,0:T(8,128)S(1)} %get-tuple-element.4) | data formatting | bytes 1179648
  36.0 0.8 %copy.11 = f32[128,1152]{1,0:T(8,128)} copy(f32[128,1152]{1,0:T(8,128)S(1)} %get-tuple-element.5) | data formatting | bytes 1179648
